TPU v7x, 32 devices: a whole 2x2x4 slice. The times are simulated.
32 devices in a mesh: tile: 16 (over z, x, core), harm: 2 (over y).
Axes of the slice: x: 2, y: 2, z: 4, core: 2. Of those that a mesh axis runs over, the one named last changes fastest.
Arguments:
- adjoint: float32 [24, 64, 320], P('harm', 'tile'), may hold values from -6 to 6
- objective_grad: float32 [24, 64, 320], P('harm', 'tile'), may hold values from -6 to 6
- first_jacobian_blocks: bfloat16 [64, 4, 320, 320], P(('tile', 'harm')), may hold values from -0.15625 to 0.15625
- second_jacobian_blocks: bfloat16 [64, 4, 320, 320], P(('tile', 'harm')), may hold values from -0.15625 to 0.15625
- block_column_layout: int32 [64, 4], P('tile'), may hold values from 0 to 11
- coupling: float32 [24, 24], replicated, may hold values from -1.25 to 1.25
- matching: int32 [64, 2], P('tile'), may hold values from 0 to 3
- intersection: float32 [64, 2], P('tile'), may hold values from 0.25 to 1
- modes: int32 [12], replicated, may hold values from -6 to 6
- clocking: float32 [64], P('tile'), may hold values from -3.140625 to 3.140625
Outputs:
- update: float32 [24, 64, 320], P('harm', 'tile')
All inputs are finite; a program needn't handle non-finite values.
Results may differ from a plain program's by a relative error of at most 0.0033.
Values may be sent and summed in bfloat16 or wider, within the bound.
A program may use at most 128 MiB of HBM per device.

v0:
```python
import jax
import jax.numpy as jnp
from jax import lax
from jax.sharding import PartitionSpec as P

VARS = 5
IF_CELLS = 8


def shifted(block, axis, distance):
    devices = range(lax.axis_size(axis))
    route = [((i - distance) % len(devices), i) for i in devices]
    return lax.ppermute(block, axis, route)


def swapped(shard, axis, bit):
    return lax.ppermute(shard, axis, [(i, i ^ 1 << bit) for i in range(lax.axis_size(axis))])


def fold_window(term_list, rows_pattern, span):
    one_hot_selector = (
        rows_pattern.reshape(-1)[:, None] == jnp.arange(span, dtype=jnp.int32)[None, :]
    ).astype(jnp.float32)
    return jnp.einsum("sop,or->srp", term_list, one_hot_selector, precision=lax.Precision.HIGHEST)


def block_products(vectors, blocks):
    heads = vectors.shape[0]
    term_list = jnp.einsum("hnc,nkcd->hnkd", vectors, blocks, preferred_element_type=jnp.float32)
    return term_list.reshape(heads, blocks.shape[0] * blocks.shape[1], blocks.shape[3])


def window_terms(vectors, blocks, rows_pattern, span):
    return fold_window(block_products(vectors, blocks), rows_pattern, span)


def spread(window, group):
    left_part = window[:, :group]
    middle = window[:, group : 2 * group]
    right_part = window[:, 2 * group :]
    from_next = shifted(left_part, "tile", -1)
    from_prev = shifted(right_part, "tile", 1)
    return middle + from_next + from_prev


def local(
    adjoint,
    objective_grad,
    first_jacobian_blocks,
    second_jacobian_blocks,
    block_column_layout,
    coupling,
    matching,
    intersection,
    modes,
    clocking,
):
    local_hc, group, width = adjoint.shape
    harm_count = lax.axis_size("harm")
    row_count = group // harm_count
    full_hc = coupling.shape[0]
    half_hc = full_hc // 2
    strip_width = IF_CELLS * VARS
    span = 3 * group
    harm_index = lax.axis_index("harm")
    own_clock = lax.dynamic_slice_in_dim(clocking, harm_index * row_count, row_count, 0)

    def split_product(vectors, jacobian_blocks):
        window = window_terms(
            vectors,
            lax.all_gather(jacobian_blocks, "harm", axis=0, tiled=True),
            block_column_layout,
            span,
        )
        return spread(window, group)

    adjoint_batch = adjoint.astype(jnp.bfloat16)
    first_operator = split_product(adjoint_batch, first_jacobian_blocks)
    strips = first_operator[:, :, :strip_width]
    top_bit = lax.axis_size("tile").bit_length() - 2
    partner_side = swapped(strips, "tile", top_bit)
    positions = jnp.arange(group, dtype=jnp.int32)[None, :]
    mortar_weight_table = intersection[:, 0:1] * (matching[:, 0:1] == positions).astype(jnp.float32)
    mortar_weight_table = mortar_weight_table + intersection[:, 1:2] * (
        matching[:, 1:2] == positions
    ).astype(jnp.float32)
    mortar_coupling = jnp.einsum(
        "au,fur->far", mortar_weight_table, partner_side, precision=lax.Precision.HIGHEST
    )
    first_all, mortar_all = (
        lax.all_to_all(first_operator, "harm", split_axis=1, concat_axis=0, tiled=True),
        lax.all_to_all(mortar_coupling, "harm", split_axis=1, concat_axis=0, tiled=True),
    )
    phi = modes.astype(jnp.float32)[:, None] * own_clock[None, :]
    cosine = jnp.cos(phi)[:, :, None]
    sine = jnp.sin(phi)[:, :, None]
    mortar_cos = mortar_all[:half_hc]
    mortar_sin = mortar_all[half_hc:]
    rotated = jnp.concatenate(
        [cosine * mortar_cos - sine * mortar_sin, sine * mortar_cos + cosine * mortar_sin], axis=0
    )
    mixed = jnp.einsum("hg,gtd->htd", coupling, first_all, precision=lax.Precision.HIGHEST)
    padded = jnp.pad(rotated, ((0, 0), (0, 0), (0, width - strip_width)))
    coupled_result = (first_all + mixed + padded).astype(jnp.bfloat16)
    coupled_split = lax.all_to_all(coupled_result, "harm", split_axis=0, concat_axis=1, tiled=True)
    second_operator = split_product(coupled_split, second_jacobian_blocks)
    return objective_grad - second_operator


def solution(mesh):
    return jax.shard_map(
        local,
        mesh=mesh,
        in_specs=(
            P("harm", "tile", None),
            P("harm", "tile", None),
            P(("tile", "harm"), None, None, None),
            P(("tile", "harm"), None, None, None),
            P("tile", None),
            P(),
            P("tile", None),
            P("tile", None),
            P(),
            P("tile"),
        ),
        out_specs=P("harm", "tile", None),
        check_vma=False,
    )
```

profile of v0, /device:TPU:0, one launch (start us, length us, event | category | flops | bytes accessed | tf_op | source)
XLA Modules:
  0.0 143.3 jit_solution(1947695084984806295)
XLA Ops:
  6.5 0.0 copy-start
  6.5 0.0 copy-start.3
  6.5 0.0 copy-start.1
  6.5 0.0 all-gather.3.cloned.1.call-start
  6.5 0.7 all-gather.3.cloned.1.call-update
  7.3 0.0 copy-start.4
  7.3 0.0 copy-start.5
  7.3 0.0 copy-start.6
  7.3 0.0 copy-start.7
  7.3 0.0 all-gather.5.cloned.1.call-start
  7.3 0.7 all-gather.5.cloned.1.call-update
  8.1 0.0 copy-done.3
  8.1 0.1 eq.24
  8.1 0.0 copy-done.1
  8.2 57.3 %all-gather.3.cloned.1.call-done = bf16[4,4,320,320]{3,2,1,0:T(8,128)(2,1)} async-done(((bf16[2,4,320,320]{3,2,1,0:T(8,128)(2,1)}), bf16[4,4,320,320]{3,2,1,0:T(8,128)(2,1)}) %all-gather.3.cloned.1.call-update) | async-done | bytes 3276816 | tf_op jit(solution)/shard_map/all_gather | solution.py:71
  65.4 2.7 %fusion.9 = f32[4,4,320,12]{2,3,1,0:T(8,128)S(1)} fusion(bf16[4,4,320,320]{3,2,1,0:T(8,128)(2,1)} %all-gather.3.cloned.1.call-done, bf16[12,4,320,1]{2,1,0,3:T(4,128)(2,1)S(1)} %convert_bitcast_fusion), kind=kOutput, calls=%fused_computation.17 | convolution fusion | flops 39321600 | bytes 3553280 | tf_op jit(solution)/shard_map/hnc,nkcd->hnkd/dot_general | solution.py:29
  68.2 0.3 convolution_bitcast_fusion.1
  68.6 3.7 %collective-permute-start = (f32[12,4,320]{2,1,0:T(4,128)S(1)}, f32[12,4,320]{2,1,0:T(4,128)S(1)}, u32[]{:S(2)}, u32[]{:S(2)}) collective-permute-start(f32[12,4,320]{2,1,0:T(4,128)S(1)} %get-tuple-element.7), channel_id=1, source_target_pairs={{2,0},{4,2},{6,4},{8,6},{10,8},{12,10},{14,12},{16,14},{18,16},{20... | collective-permute-start | bytes 184328 | tf_op jit(solution)/shard_map/ppermute | solution.py:13
  72.3 0.0 collective-permute-start.1
  72.3 0.0 copy-done.4
  72.3 2.0 %collective-permute-done = f32[12,4,320]{2,1,0:T(4,128)S(1)} collective-permute-done((f32[12,4,320]{2,1,0:T(4,128)S(1)}, f32[12,4,320]{2,1,0:T(4,128)S(1)}, u32[]{:S(2)}, u32[]{:S(2)}) %collective-permute-start) | collective-permute-done | bytes 61472 | tf_op jit(solution)/shard_map/ppermute | solution.py:13
  74.3 4.6 %collective-permute-done.1 = f32[12,4,320]{2,1,0:T(4,128)S(1)} collective-permute-done((f32[12,4,320]{2,1,0:T(4,128)S(1)}, f32[12,4,320]{2,1,0:T(4,128)S(1)}, u32[]{:S(2)}, u32[]{:S(2)}) %collective-permute-start.1) | collective-permute-done | bytes 61472 | tf_op jit(solution)/shard_map/ppermute | solution.py:13
  78.9 0.1 collective-permute-start.2
  79.0 0.0 copy-done.5
  79.0 0.0 copy-done.6
  79.0 0.0 copy-done.7
  79.1 0.1 dynamic_slice.3
  79.1 4.6 %collective-permute-done.2 = f32[12,4,40]{2,1,0:T(4,128)S(1)} collective-permute-done((f32[12,4,40]{2,1,0:T(4,128)S(1)}, f32[12,4,40]{2,1,0:T(4,128)S(1)}, u32[]{:S(2)}, u32[]{:S(2)}) %collective-permute-start.2) | collective-permute-done | bytes 7712 | tf_op jit(solution)/shard_map/ppermute | solution.py:17
  83.7 0.2 convolution_bitcast_fusion.3
  84.0 0.7 reshape.67
  84.7 3.2 %all-to-all-start.1 = ((f32[2,1,960]{2,1,0:T(1,128)}), f32[2,1,960]{2,1,0:T(1,128)S(1)}, u32[]{:S(2)}, u32[]{:S(2)}) async-start(f32[2,1,960]{2,1,0:T(1,128)} %reshape.67), calls=%async_computation.1 | async-start | bytes 16384 | tf_op jit(solution)/shard_map/all_to_all | solution.py:92
  87.9 0.1 multiply_cosine_fusion
  88.0 0.6 copy.28
  88.6 3.1 %all-to-all-done.1 = f32[2,1,960]{2,1,0:T(1,128)S(1)} async-done(((f32[2,1,960]{2,1,0:T(1,128)}), f32[2,1,960]{2,1,0:T(1,128)S(1)}, u32[]{:S(2)}, u32[]{:S(2)}) %all-to-all-start.1) | async-done | bytes 7712 | tf_op jit(solution)/shard_map/all_to_all | solution.py:92
  91.8 3.3 %all-to-all-start = ((f32[12,4,320]{2,0,1:T(8,128)}), f32[12,4,320]{2,0,1:T(8,128)S(1)}, u32[]{:S(2)}, u32[]{:S(2)}) async-start(f32[12,4,320]{2,0,1:T(8,128)} %copy.28), calls=%async_computation | async-start | bytes 196608 | tf_op jit(solution)/shard_map/all_to_all | solution.py:91
  95.1 0.5 broadcast.53
  95.6 0.7 reduce
  96.3 0.1 reshape.68
  96.4 0.1 multiply_subtract_fusion
  96.5 3.9 %all-to-all-done = f32[12,4,320]{2,0,1:T(8,128)S(1)} async-done(((f32[12,4,320]{2,0,1:T(8,128)}), f32[12,4,320]{2,0,1:T(8,128)S(1)}, u32[]{:S(2)}, u32[]{:S(2)}) %all-to-all-start) | async-done | bytes 61472 | tf_op jit(solution)/shard_map/all_to_all | solution.py:91
  100.5 0.0 copy-done
  100.5 0.0 copy-start.2
  100.5 0.2 fusion.2
  100.7 6.7 %all_to_all.51 = bf16[24,2,320]{2,1,0:T(2,128)(2,1)S(1)} all-to-all(bf16[24,2,320]{2,1,0:T(2,128)(2,1)S(1)} %copy.33), channel_id=1, replica_groups=mesh['tile'=16,'harm'=2] {'harm'}, dimensions={0} | all-to-all | bytes 61440 | tf_op jit(solution)/shard_map/all_to_all | solution.py:105
  107.4 14.9 %all-gather.5.cloned.1.call-done = bf16[4,4,320,320]{3,2,1,0:T(8,128)(2,1)} async-done(((bf16[2,4,320,320]{3,2,1,0:T(8,128)(2,1)}), bf16[4,4,320,320]{3,2,1,0:T(8,128)(2,1)}) %all-gather.5.cloned.1.call-update) | async-done | bytes 3276816 | tf_op jit(solution)/shard_map/all_gather | solution.py:71
  122.3 2.8 %fusion.29 = f32[4,12,4,320]{3,1,2,0:T(8,128)S(1)} fusion(bf16[12,4,320,1]{2,0,3,1:T(8,128)(2,1)S(1)} %bitcast.78, bf16[4,4,320,320]{3,2,1,0:T(8,128)(2,1)} %all-gather.5.cloned.1.call-done), kind=kOutput, calls=%fused_computation.50 | convolution fusion | flops 39321600 | bytes 3553280 | tf_op jit(solution)/shard_map/hnc,nkcd->hnkd/dot_general | solution.py:29
  125.2 0.3 convolution_bitcast_fusion
  125.5 3.7 %collective-permute-start.3 = (f32[12,4,320]{2,1,0:T(4,128)S(1)}, f32[12,4,320]{2,1,0:T(4,128)S(1)}, u32[]{:S(2)}, u32[]{:S(2)}) collective-permute-start(f32[12,4,320]{2,1,0:T(4,128)S(1)} %get-tuple-element.5), channel_id=1, source_target_pairs={{2,0},{4,2},{6,4},{8,6},{10,8},{12,10},{14,12},{16,14},{18,16},{20... | collective-permute-start | bytes 184328 | tf_op jit(solution)/shard_map/ppermute | solution.py:13
  129.3 0.0 collective-permute-start.4
  129.3 2.0 %collective-permute-done.3 = f32[12,4,320]{2,1,0:T(4,128)S(1)} collective-permute-done((f32[12,4,320]{2,1,0:T(4,128)S(1)}, f32[12,4,320]{2,1,0:T(4,128)S(1)}, u32[]{:S(2)}, u32[]{:S(2)}) %collective-permute-start.3) | collective-permute-done | bytes 61472 | tf_op jit(solution)/shard_map/ppermute | solution.py:13
  131.2 4.5 %collective-permute-done.4 = f32[12,4,320]{2,1,0:T(4,128)S(1)} collective-permute-done((f32[12,4,320]{2,1,0:T(4,128)S(1)}, f32[12,4,320]{2,1,0:T(4,128)S(1)}, u32[]{:S(2)}, u32[]{:S(2)}) %collective-permute-start.4) | collective-permute-done | bytes 61472 | tf_op jit(solution)/shard_map/ppermute | solution.py:13
  135.7 0.0 copy-done.2
  135.7 0.7 fusion.6
  (12 shorter events, 0.2 us)
Async XLA Ops:
  6.5 93.9 %copy-start = (f32[24,24]{1,0:T(8,128)S(1)}, f32[24,24]{1,0:T(8,128)}, u32[]{:S(2)}) copy-start(f32[24,24]{1,0:T(8,128)} %param.15) | copy-start | bytes 6916
  6.5 1.5 %copy-start.3 = (s32[4,4]{1,0:T(4,128)S(1)}, s32[4,4]{1,0:T(4,128)}, u32[]{:S(2)}) copy-start(s32[4,4]{1,0:T(4,128)} %param.14) | copy-start | bytes 196
  6.5 1.6 %copy-start.1 = (f32[12,4,320]{2,1,0:T(4,128)S(1)}, f32[12,4,320]{2,1,0:T(4,128)}, u32[]{:S(2)}) copy-start(f32[12,4,320]{2,1,0:T(4,128)} %param.10) | copy-start | bytes 184324
  6.5 58.9 %all-gather.3.cloned.1.call-start = ((), (), s32[]{:S(2)}) async-start(), calls=%async_computation.3 | async-start | bytes 5898240 | tf_op jit(solution)/shard_map/all_gather | solution.py:71
  7.3 65.0 %copy-start.4 = (s32[4,2]{0,1:T(2,128)S(1)}, s32[4,2]{0,1:T(2,128)}, u32[]{:S(2)}) copy-start(s32[4,2]{0,1:T(2,128)} %param.16) | copy-start | bytes 100
  7.3 71.7 %copy-start.5 = (f32[4,2]{0,1:T(2,128)S(1)}, f32[4,2]{0,1:T(2,128)}, u32[]{:S(2)}) copy-start(f32[4,2]{0,1:T(2,128)} %param.17) | copy-start | bytes 100
  7.3 71.7 %copy-start.6 = (s32[12]{0:T(128)S(1)}, s32[12]{0:T(128)}, u32[]{:S(2)}) copy-start(s32[12]{0:T(128)} %param.18) | copy-start | bytes 148
  7.3 71.8 %copy-start.7 = (f32[4]{0:T(128)S(1)}, f32[4]{0:T(128)}, u32[]{:S(2)}) copy-start(f32[4]{0:T(128)} %param.19) | copy-start | bytes 52
  7.3 115.0 %all-gather.5.cloned.1.call-start = ((), (), s32[]{:S(2)}) async-start(), calls=%async_computation.4 | async-start | bytes 5898240 | tf_op jit(solution)/shard_map/all_gather | solution.py:71
  68.6 5.7 %collective-permute-start = (f32[12,4,320]{2,1,0:T(4,128)S(1)}, f32[12,4,320]{2,1,0:T(4,128)S(1)}, u32[]{:S(2)}, u32[]{:S(2)}) collective-permute-start(f32[12,4,320]{2,1,0:T(4,128)S(1)} %get-tuple-element.7), channel_id=1, source_target_pairs={{2,0},{4,2},{6,4},{8,6},{10,8},{12,10},{14,12},{16,14},{18,16},{20... | collective-permute-start | bytes 184328 | tf_op jit(solution)/shard_map/ppermute | solution.py:13
  72.3 6.6 %collective-permute-start.1 = (f32[12,4,320]{2,1,0:T(4,128)S(1)}, f32[12,4,320]{2,1,0:T(4,128)S(1)}, u32[]{:S(2)}, u32[]{:S(2)}) collective-permute-start(f32[12,4,320]{2,1,0:T(4,128)S(1)} %get-tuple-element.8), channel_id=1, source_target_pairs={{30,0},{0,2},{2,4},{4,6},{6,8},{8,10},{10,12},{12,14},{14,16},{16,... | collective-permute-start | bytes 184328 | tf_op jit(solution)/shard_map/ppermute | solution.py:13
  78.9 4.8 %collective-permute-start.2 = (f32[12,4,40]{2,1,0:T(4,128)S(1)}, f32[12,4,40]{2,1,0:T(4,128)S(1)}, u32[]{:S(2)}, u32[]{:S(2)}) collective-permute-start(f32[12,4,40]{2,1,0:T(4,128)S(1)} %slice.63), channel_id=1, source_target_pairs={{0,16},{2,18},{4,20},{6,22},{8,24},{10,26},{12,28},{14,30},{16,0},... | collective-permute-start | bytes 23048 | tf_op jit(solution)/shard_map/ppermute | solution.py:17
  84.7 7.1 %all-to-all-start.1 = ((f32[2,1,960]{2,1,0:T(1,128)}), f32[2,1,960]{2,1,0:T(1,128)S(1)}, u32[]{:S(2)}, u32[]{:S(2)}) async-start(f32[2,1,960]{2,1,0:T(1,128)} %reshape.67), calls=%async_computation.1 | async-start | bytes 16384 | tf_op jit(solution)/shard_map/all_to_all | solution.py:92
  91.8 8.7 %all-to-all-start = ((f32[12,4,320]{2,0,1:T(8,128)}), f32[12,4,320]{2,0,1:T(8,128)S(1)}, u32[]{:S(2)}, u32[]{:S(2)}) async-start(f32[12,4,320]{2,0,1:T(8,128)} %copy.28), calls=%async_computation | async-start | bytes 196608 | tf_op jit(solution)/shard_map/all_to_all | solution.py:91
  100.5 35.3 %copy-start.2 = (f32[12,4,320]{2,1,0:T(4,128)S(1)}, f32[12,4,320]{2,1,0:T(4,128)}, u32[]{:S(2)}) copy-start(f32[12,4,320]{2,1,0:T(4,128)} %param.11) | copy-start | bytes 184324
  125.5 5.7 %collective-permute-start.3 = (f32[12,4,320]{2,1,0:T(4,128)S(1)}, f32[12,4,320]{2,1,0:T(4,128)S(1)}, u32[]{:S(2)}, u32[]{:S(2)}) collective-permute-start(f32[12,4,320]{2,1,0:T(4,128)S(1)} %get-tuple-element.5), channel_id=1, source_target_pairs={{2,0},{4,2},{6,4},{8,6},{10,8},{12,10},{14,12},{16,14},{18,16},{20... | collective-permute-start | bytes 184328 | tf_op jit(solution)/shard_map/ppermute | solution.py:13
  129.3 6.5 %collective-permute-start.4 = (f32[12,4,320]{2,1,0:T(4,128)S(1)}, f32[12,4,320]{2,1,0:T(4,128)S(1)}, u32[]{:S(2)}, u32[]{:S(2)}) collective-permute-start(f32[12,4,320]{2,1,0:T(4,128)S(1)} %get-tuple-element.6), channel_id=1, source_target_pairs={{30,0},{0,2},{2,4},{4,6},{6,8},{8,10},{10,12},{12,14},{14,16},{16,... | collective-permute-start | bytes 184328 | tf_op jit(solution)/shard_map/ppermute | solution.py:13
Sparse Core Ops, SparseCore 0:
  8.9 56.4 all-gather.2
  67.0 55.3 all-gather.4
where the time goes:
time: 144 us; the launch traced here: 143 us
  waiting for transfers between devices  98.3 us (68%)
  starting transfers between devices  14.1 us (10%)
  between operations  13.6 us (9%)
  blocking collectives  6.69 us (5%)
  matrix products  6.68 us (5%)
  local copies, waits for them, and re-layouts  2.27 us (2%)
  other arithmetic  1.59 us (1%)
    all_gather x2, waiting for transfers between devices, split_product(): lax.all_gather(jacobian_blocks, 'harm', axis=0, tiled=True)  72.2 us
    ppermute x4, waiting for transfers between devices, shifted(): return lax.ppermute(block, axis, route)  13 us
    ppermute x4, starting transfers between devices, shifted(): return lax.ppermute(block, axis, route)  7.45 us
    all_to_all x1, blocking collectives, local(): lax.all_to_all(coupled_result, 'harm', split_axis=0, concat_axis=1, tiled...  6.69 us
    dot_general x2, matrix products, block_products(): jnp.einsum('hnc,nkcd->hnkd', vectors, blocks, preferred_element_type=jnp....  5.55 us
    ppermute x1, waiting for transfers between devices, swapped(): lax.ppermute(shard, axis, [(i, i ^ 1 << bit) for i in range(lax.axis_size...  4.57 us
    all_to_all x1, waiting for transfers between devices, local(): lax.all_to_all(first_operator, 'harm', split_axis=1, concat_axis=0, tiled...  3.95 us
    all_to_all x1, starting transfers between devices, local(): lax.all_to_all(first_operator, 'harm', split_axis=1, concat_axis=0, tiled...  3.34 us
  transfers between devices with their start and end apart: 9, of which 9 were waited for; matrix products, arithmetic and copies ran while one was open for 5% of the time, Pallas kernels for 0%

commit v1 on v0

v1 whole, which is shorter than its diff:
```python
import functools

import jax
import jax.numpy as jnp
from jax import lax
from jax.experimental import pallas as pl
from jax.experimental.pallas import tpu as pltpu
from jax.sharding import PartitionSpec as P

VARS = 5
IF_CELLS = 8
STRIP = VARS * IF_CELLS
LANES = 128
MESH = pl.DeviceIdType.MESH


def kernel(
    tiles,
    harms,
    adj,
    layout,
    coupling,
    matching,
    weights,
    modes,
    clocking,
    first_hbm,
    second_hbm,
    out,
    first_j,
    second_j,
    pad,
    a_send,
    a_recv,
    full,
    terms,
    send1,
    recv1,
    m_send,
    m_recv,
    swap,
    send2,
    recv2,
    j1_sem,
    j2_sem,
    a_ssem,
    a_rsem,
    s1_sem,
    r1_sem,
    m_ssem,
    m_rsem,
    s2_sem,
    r2_sem,
):
    my_t = lax.axis_index("tile")
    my_h = lax.axis_index("harm")
    own_hc, group, width = adj.shape
    rows, kk = first_j.shape[0], first_j.shape[1]
    hc = coupling.shape[0]
    half = hc // 2
    base = my_h * rows
    far = lax.rem(my_t + tiles // 2, tiles)
    near = [lax.rem(my_t + tiles - 1, tiles), my_t, lax.rem(my_t + 1, tiles)]

    def block_copies(hbm, vmem, sem):
        return [
            pltpu.make_async_copy(hbm.at[r, k], vmem.at[r, k], sem.at[r * kk + k])
            for r in range(rows)
            for k in range(kk)
        ]

    first_copies = block_copies(first_hbm, first_j, j1_sem)
    second_copies = block_copies(second_hbm, second_j, j2_sem)
    for copy in first_copies:
        copy.start()

    barrier = pltpu.get_barrier_semaphore()
    for d in (-1, 0, 1):
        for h in range(harms):
            if d == 0:
                @pl.when(h != my_h)
                def _():
                    pl.semaphore_signal(barrier, inc=1, device_id=(my_t, h), device_id_type=MESH)
            else:
                pl.semaphore_signal(barrier, inc=1, device_id=(near[d + 1], h), device_id_type=MESH)
    for h in range(harms):
        pl.semaphore_signal(barrier, inc=1, device_id=(far, h), device_id_type=MESH)

    pad[...] = jnp.zeros_like(pad)
    for h in range(harms):
        for r in range(rows):
            pad[h * rows + r, 0:own_hc, :] = adj[:, h * rows + r, :]
    for h in range(harms):
        for r in range(rows):
            a_send[h, r] = pad[h * rows + r].astype(jnp.bfloat16)

    pl.semaphore_wait(barrier, 4 * harms - 1)

    def a_copy(to, slot, sem):
        return pltpu.make_async_remote_copy(
            src_ref=a_send.at[to],
            dst_ref=a_recv.at[slot],
            send_sem=a_ssem.at[to],
            recv_sem=a_rsem.at[sem],
            device_id=(my_t, to),
            device_id_type=MESH,
        )

    def other(h):
        return h != my_h

    for h in range(harms):
        @pl.when(other(h))
        def _():
            a_copy(h, my_h, my_h).start()

    for copy in second_copies:
        copy.start()

    a_recv[my_h] = a_send[my_h]

    row_id = lax.broadcasted_iota(jnp.int32, (hc, LANES), 0)
    lane_id = lax.broadcasted_iota(jnp.int32, (hc, LANES), 1)
    mode = jnp.zeros((hc, LANES), jnp.float32)
    for n in range(half):
        value = modes[n].astype(jnp.float32)
        mode = jnp.where((row_id == n) | (row_id == n + half), value, mode)
    cosines, sines = [], []
    for r in range(rows):
        phi = mode * clocking[base + r]
        inside = lane_id < STRIP
        sine = jnp.sin(phi)
        cosines.append(jnp.where(inside, jnp.cos(phi), 0.0))
        sines.append(jnp.where(inside, jnp.where(row_id < half, -sine, sine), 0.0))

    spot = [[layout[base + r, k] for k in range(kk)] for r in range(rows)]

    def one(r, k, slot):
        return jnp.where(spot[r][k] == slot, 1.0, 0.0).astype(jnp.float32)

    def fold(slot):
        total = None
        for r in range(rows):
            for k in range(kk):
                term = one(r, k, slot) * terms[r * kk + k]
                total = term if total is None else total + term
        return total

    for h in range(harms):
        @pl.when(other(h))
        def _():
            a_copy(h, h, h).wait_recv()
    for r in range(rows):
        for h in range(harms):
            full[r, h * own_hc : (h + 1) * own_hc, :] = a_recv[h, r].astype(jnp.float32)[0:own_hc]

    def products(vectors, blocks, copies):
        for r in range(rows):
            for k in range(kk):
                copies[r * kk + k].wait()
                terms[r * kk + k] = jnp.dot(
                    vectors[r], blocks[r, k], preferred_element_type=jnp.float32
                )

    def exchange(send, recv, ssem, rsem):
        def copy(d, to, slot):
            return pltpu.make_async_remote_copy(
                src_ref=send.at[(d + 1) * harms + to],
                dst_ref=recv.at[slot],
                send_sem=ssem.at[(d + 1) * harms + to],
                recv_sem=rsem.at[slot],
                device_id=(near[d + 1], to),
                device_id_type=MESH,
            )

        def start(d, to):
            if d == 0:
                @pl.when(other(to))
                def _():
                    copy(d, to, harms + my_h).start()
            else:
                copy(d, to, (d + 1) * harms + my_h).start()

        def finish(d, h):
            if d == 0:
                @pl.when(other(h))
                def _():
                    copy(d, h, harms + h).wait_recv()
            else:
                copy(d, h, (d + 1) * harms + h).wait_recv()

        def drain():
            for d in (-1, 0, 1):
                for h in range(harms):
                    if d == 0:
                        @pl.when(other(h))
                        def _():
                            copy(d, h, harms + h).wait_send()
                    else:
                        copy(d, h, (d + 1) * harms + h).wait_send()

        def collect():
            total = send[harms + my_h]
            for d in (-1, 1, 0):
                for h in range(harms):
                    finish(d, h)
                if d == 0:
                    for j in range(1, harms):
                        total = total + recv[harms + lax.rem(my_h + j, harms)]
                else:
                    for h in range(harms):
                        total = total + recv[(d + 1) * harms + h]
            return total

        return start, collect, drain

    start1, collect1, drain1 = exchange(send1, recv1, s1_sem, r1_sem)
    start2, collect2, drain2 = exchange(send2, recv2, s2_sem, r2_sem)

    products([full[r].astype(jnp.bfloat16) for r in range(rows)], first_j, first_copies)
    for d in (-1, 1, 0):
        for h in range(harms):
            for r in range(rows):
                send1[(d + 1) * harms + h, r] = fold((d + 1) * group + h * rows + r)
            start1(d, h)
    first = collect1()

    m_send[...] = first[:, :, 0:LANES]

    def m_copy(to, slot):
        return pltpu.make_async_remote_copy(
            src_ref=m_send,
            dst_ref=m_recv.at[slot],
            send_sem=m_ssem.at[to],
            recv_sem=m_rsem.at[slot],
            device_id=(far, to),
            device_id_type=MESH,
        )

    for h in range(harms):
        m_copy(h, my_h).start()
    plain = []
    for r in range(rows):
        plain.append(
            first[r]
            + jnp.dot(
                coupling[...],
                first[r],
                precision=lax.Precision.HIGHEST,
                preferred_element_type=jnp.float32,
            )
        )
    for h in range(harms):
        m_copy(h, h).wait_recv()
    coupled = []
    for r in range(rows):
        mortar = jnp.zeros((hc, LANES), jnp.float32)
        for h in range(harms):
            for q in range(rows):
                place = h * rows + q
                weight = jnp.where(matching[base + r, 0] == place, weights[base + r, 0], 0.0)
                weight = weight + jnp.where(matching[base + r, 1] == place, weights[base + r, 1], 0.0)
                mortar = mortar + weight * m_recv[h, q]
        swap[r, 0:half, :] = mortar[half:]
        swap[r, half:, :] = mortar[0:half]
        rotated = cosines[r] * mortar + sines[r] * swap[r]
        head = plain[r][:, 0:LANES] + rotated
        coupled.append(
            jnp.concatenate([head, plain[r][:, LANES:]], axis=1).astype(jnp.bfloat16)
        )

    products(coupled, second_j, second_copies)
    for d in (-1, 1, 0):
        for s in range(group):
            value = fold((d + 1) * group + s)
            for h in range(harms):
                send2[(d + 1) * harms + h, s * own_hc : (s + 1) * own_hc, :] = value[
                    h * own_hc : (h + 1) * own_hc
                ]
        for h in range(harms):
            start2(d, h)
    out[...] = collect2()

    for h in range(harms):
        @pl.when(other(h))
        def _():
            a_copy(h, h, h).wait_send()
        m_copy(h, h).wait_send()
    drain1()
    drain2()


def local(
    tiles,
    harms,
    adjoint,
    objective_grad,
    first_jacobian_blocks,
    second_jacobian_blocks,
    block_column_layout,
    coupling,
    matching,
    intersection,
    modes,
    clocking,
):
    own_hc, group, width = adjoint.shape
    rows, kk = first_jacobian_blocks.shape[:2]
    hc = coupling.shape[0]
    padded = -(-own_hc // 16) * 16
    vmem = pl.BlockSpec(memory_space=pltpu.VMEM)
    smem = pl.BlockSpec(memory_space=pltpu.SMEM)
    hbm = pl.BlockSpec(memory_space=pl.ANY)
    f32, bf16 = jnp.float32, jnp.bfloat16
    dma = pltpu.SemaphoreType.DMA
    second = pl.pallas_call(
        functools.partial(kernel, tiles, harms),
        out_shape=jax.ShapeDtypeStruct((group * own_hc, width), f32),
        in_specs=[vmem, smem, vmem, smem, smem, smem, smem, hbm, hbm],
        out_specs=vmem,
        scratch_shapes=[
            pltpu.VMEM(first_jacobian_blocks.shape, bf16),
            pltpu.VMEM(first_jacobian_blocks.shape, bf16),
            pltpu.VMEM((group, padded, width), f32),
            pltpu.VMEM((harms, rows, padded, width), bf16),
            pltpu.VMEM((harms, rows, padded, width), bf16),
            pltpu.VMEM((rows, hc, width), f32),
            pltpu.VMEM((rows * kk, hc, width), f32),
            pltpu.VMEM((3 * harms, rows, hc, width), f32),
            pltpu.VMEM((3 * harms, rows, hc, width), f32),
            pltpu.VMEM((rows, hc, LANES), f32),
            pltpu.VMEM((harms, rows, hc, LANES), f32),
            pltpu.VMEM((rows, hc, LANES), f32),
            pltpu.VMEM((3 * harms, group * own_hc, width), f32),
            pltpu.VMEM((3 * harms, group * own_hc, width), f32),
            dma((rows * kk,)),
            dma((rows * kk,)),
            dma((harms,)),
            dma((harms,)),
            dma((3 * harms,)),
            dma((3 * harms,)),
            dma((harms,)),
            dma((harms,)),
            dma((3 * harms,)),
            dma((3 * harms,)),
        ],
        compiler_params=pltpu.CompilerParams(
            collective_id=0, has_side_effects=True, vmem_limit_bytes=40 * 1024 * 1024
        ),
    )(
        adjoint,
        block_column_layout,
        coupling,
        matching,
        intersection,
        modes,
        clocking,
        first_jacobian_blocks,
        second_jacobian_blocks,
    )
    return objective_grad - jnp.transpose(second.reshape(group, own_hc, width), (1, 0, 2))


def solution(mesh):
    return jax.shard_map(
        functools.partial(local, mesh.shape["tile"], mesh.shape["harm"]),
        mesh=mesh,
        in_specs=(
            P("harm", "tile", None),
            P("harm", "tile", None),
            P(("tile", "harm"), None, None, None),
            P(("tile", "harm"), None, None, None),
            P("tile", None),
            P(),
            P("tile", None),
            P("tile", None),
            P(),
            P("tile"),
        ),
        out_specs=P("harm", "tile", None),
        check_vma=False,
    )
```

time: 144 us -> 39.6 us (0.28)
  waiting for transfers between devices: 98.3 us -> 0 us
  Pallas kernels: 0 us -> 30.3 us
  starting transfers between devices: 14.1 us -> 0 us
  between operations: 13.6 us -> 0.04 us
  blocking collectives: 6.69 us -> 0 us
  matrix products: 6.68 us -> 0 us
  local copies, waits for them, and re-layouts: 2.27 us -> 8.87 us
  other arithmetic: 1.59 us -> 0.02 us
    all_gather x2 -> x0, waiting for transfers between devices: 72.2 us -> none  [split_product(): lax.all_gather(jacobian_blocks, 'harm', axis=0, tiled=True)]
    pallas_call x0 -> x1, Pallas kernels: none -> 30.3 us  [local(): pl.pallas_call(functools.partial(kernel, tiles, harms), out_shape=jax.Sha...]
    ppermute x5 -> x0, waiting for transfers between devices: 17.6 us -> none  [the longest x4 13 us: shifted(): return lax.ppermute(block, axis, route)]
    ppermute x5 -> x0, starting transfers between devices: 7.52 us -> none  [the longest x4 7.45 us: shifted(): return lax.ppermute(block, axis, route)]
    unnamed x18, local copies, waits for them, and re-layouts: 0.81 us -> 8.2 us
    all_to_all x2 -> x0, waiting for transfers between devices: 7.08 us -> none  [the longest x1 3.95 us: local(): lax.all_to_all(first_operator, 'harm', split_axis=1, concat_axis=0, tiled...]
    all_to_all x1 -> x0, blocking collectives: 6.69 us -> none  [local(): lax.all_to_all(coupled_result, 'harm', split_axis=0, concat_axis=1, tiled...]
    dot_general x6 -> x0, matrix products: 6.68 us -> none  [the longest x2 5.55 us: block_products(): jnp.einsum('hnc,nkcd->hnkd', vectors, blocks, preferred_element_type=jnp....]
  transfers between devices with their start and end apart: 9 -> 0, of which waited for: 9 -> 0; matrix products, arithmetic and copies ran while one was open for 5% -> 0% of each run, Pallas kernels for 0% -> 0%
where the time goes in v1:
time: 39.6 us; the launch traced here: 39.3 us
  Pallas kernels  30.3 us (77%)
  local copies, waits for them, and re-layouts  8.87 us (22%)
    pallas_call x1, Pallas kernels, local(): pl.pallas_call(functools.partial(kernel, tiles, harms), out_shape=jax.Sha...  30.3 us
    unnamed x18, local copies, waits for them, and re-layouts  8.2 us

profile of v1, /device:TPU:0, one launch (start us, length us, event | category | flops | bytes accessed | tf_op | source)
XLA Modules:
  0.0 39.3 jit_solution(17561382913468259001)
XLA Ops:
  0.0 0.8 %copy.14.matching = s32[4,2]{1,0:T(4,128)S(1)} copy(s32[4,2]{0,1:T(2,128)} %param.16) | data formatting | bytes 64 | tf_op args[6]
  0.8 0.8 %copy.15.weights = f32[4,2]{1,0:T(4,128)S(1)} copy(f32[4,2]{0,1:T(2,128)} %param.17) | data formatting | bytes 64 | tf_op args[7]
  1.5 0.0 copy-start
  1.5 1.5 %copy-done = bf16[2,4,320,320]{3,2,1,0:T(8,128)(2,1)S(1)} copy-done((bf16[2,4,320,320]{3,2,1,0:T(8,128)(2,1)S(1)}, bf16[2,4,320,320]{3,2,1,0:T(8,128)(2,1)}, u32[]{:S(2)}) %copy-start) | copy-done | bytes 1638424
  3.1 0.0 copy-start.1
  3.1 1.5 %copy-done.1 = bf16[2,4,320,320]{3,2,1,0:T(8,128)(2,1)S(1)} copy-done((bf16[2,4,320,320]{3,2,1,0:T(8,128)(2,1)S(1)}, bf16[2,4,320,320]{3,2,1,0:T(8,128)(2,1)}, u32[]{:S(2)}) %copy-start.1) | copy-done | bytes 1638424
  4.6 0.0 copy-start.2
  4.6 0.9 %copy-done.2 = f32[12,4,320]{2,1,0:T(4,128)S(1)} copy-done((f32[12,4,320]{2,1,0:T(4,128)S(1)}, f32[12,4,320]{2,1,0:T(4,128)}, u32[]{:S(2)}) %copy-start.2) | copy-done | bytes 61464
  5.5 0.0 copy-start.3
  5.5 0.7 %copy-done.3 = f32[24,24]{1,0:T(8,128)S(1)} copy-done((f32[24,24]{1,0:T(8,128)S(1)}, f32[24,24]{1,0:T(8,128)}, u32[]{:S(2)}) %copy-start.3) | copy-done | bytes 2328
  6.2 0.0 copy-start.4
  6.2 0.7 %copy-done.4 = s32[4,4]{1,0:T(4,128)S(1)} copy-done((s32[4,4]{1,0:T(4,128)S(1)}, s32[4,4]{1,0:T(4,128)}, u32[]{:S(2)}) %copy-start.4) | copy-done | bytes 88
  6.9 0.0 copy-start.5
  6.9 0.7 %copy-done.5 = s32[12]{0:T(128)S(1)} copy-done((s32[12]{0:T(128)S(1)}, s32[12]{0:T(128)}, u32[]{:S(2)}) %copy-start.5) | copy-done | bytes 72
  7.6 0.0 copy-start.6
  7.6 0.7 %copy-done.6 = f32[4]{0:T(128)S(1)} copy-done((f32[4]{0:T(128)S(1)}, f32[4]{0:T(128)}, u32[]{:S(2)}) %copy-start.6) | copy-done | bytes 40
  8.2 0.0 copy-start.7
  8.2 30.3 %shard_map.100 = f32[48,320]{1,0:T(8,128)S(1)} custom-call(f32[12,4,320]{2,1,0:T(4,128)S(1)} %copy-done.2, s32[4,4]{1,0:T(4,128)S(1)} %copy-done.4, f32[24,24]{1,0:T(8,128)S(1)} %copy-done.3, s32[4,2]{1,0:T(4,128)S(1)} %copy.14.matching, f32[4,2]{1,0:T(4,128)S(1)} %copy.15.weights, s32[12]{0:T(128)S(1)} %copy-done.5, f32[4]{0:T(128)S(1)} %copy-done.6, ...), custom_call_target="tpu_custom_call" | custom-call | tf_op jit(solution)/shard_map/pallas_call | solution.py:316
  38.6 0.0 copy-done.7
  38.6 0.7 %copy.17 = f32[12,4,320]{2,1,0:T(4,128)} copy(f32[12,4,320]{2,0,1:T(8,128)S(1)} %bitcast_subtract_fusion) | data formatting | bytes 122880 | tf_op jit(solution)/shard_map/sub | solution.py:361
  (2 shorter events, 0.0 us)
Async XLA Ops:
  1.5 1.5 %copy-start = (bf16[2,4,320,320]{3,2,1,0:T(8,128)(2,1)S(1)}, bf16[2,4,320,320]{3,2,1,0:T(8,128)(2,1)}, u32[]{:S(2)}) copy-start(bf16[2,4,320,320]{3,2,1,0:T(8,128)(2,1)} %first_hbm.1) | copy-start | bytes 4915204
  3.1 1.5 %copy-start.1 = (bf16[2,4,320,320]{3,2,1,0:T(8,128)(2,1)S(1)}, bf16[2,4,320,320]{3,2,1,0:T(8,128)(2,1)}, u32[]{:S(2)}) copy-start(bf16[2,4,320,320]{3,2,1,0:T(8,128)(2,1)} %second_hbm.1) | copy-start | bytes 4915204
  4.6 0.9 %copy-start.2 = (f32[12,4,320]{2,1,0:T(4,128)S(1)}, f32[12,4,320]{2,1,0:T(4,128)}, u32[]{:S(2)}) copy-start(f32[12,4,320]{2,1,0:T(4,128)} %adj.1) | copy-start | bytes 184324
  5.5 0.7 %copy-start.3 = (f32[24,24]{1,0:T(8,128)S(1)}, f32[24,24]{1,0:T(8,128)}, u32[]{:S(2)}) copy-start(f32[24,24]{1,0:T(8,128)} %coupling.1) | copy-start | bytes 6916
  6.2 0.7 %copy-start.4 = (s32[4,4]{1,0:T(4,128)S(1)}, s32[4,4]{1,0:T(4,128)}, u32[]{:S(2)}) copy-start(s32[4,4]{1,0:T(4,128)} %layout.1) | copy-start | bytes 196
  6.9 0.7 %copy-start.5 = (s32[12]{0:T(128)S(1)}, s32[12]{0:T(128)}, u32[]{:S(2)}) copy-start(s32[12]{0:T(128)} %modes.1) | copy-start | bytes 148
  7.6 0.7 %copy-start.6 = (f32[4]{0:T(128)S(1)}, f32[4]{0:T(128)}, u32[]{:S(2)}) copy-start(f32[4]{0:T(128)} %clocking.1) | copy-start | bytes 52
  8.2 30.4 %copy-start.7 = (f32[12,4,320]{2,1,0:T(4,128)S(1)}, f32[12,4,320]{2,1,0:T(4,128)}, u32[]{:S(2)}) copy-start(f32[12,4,320]{2,1,0:T(4,128)} %param.11) | copy-start | bytes 184324

commit v2 on v1

--- a/solution.py
+++ b/solution.py
@@ -11,12 +11,23 @@
 IF_CELLS = 8
 STRIP = VARS * IF_CELLS
 LANES = 128
+VMEM_BYTES = 62 * 1024 * 1024
 MESH = pl.DeviceIdType.MESH
 
 
 def kernel(
     tiles,
     harms,
+    adj_hbm,
+    layout_hbm,
+    coupling_hbm,
+    matching_hbm,
+    weights_hbm,
+    modes_hbm,
+    clocking_hbm,
+    first_hbm,
+    second_hbm,
+    out,
     adj,
     layout,
     coupling,
@@ -24,9 +35,6 @@
     weights,
     modes,
     clocking,
-    first_hbm,
-    second_hbm,
-    out,
     first_j,
     second_j,
     pad,
@@ -41,6 +49,7 @@
     swap,
     send2,
     recv2,
+    in_sem,
     j1_sem,
     j2_sem,
     a_ssem,
@@ -71,6 +80,20 @@
 
     first_copies = block_copies(first_hbm, first_j, j1_sem)
     second_copies = block_copies(second_hbm, second_j, j2_sem)
+    pairs = [
+        (adj_hbm, adj),
+        (layout_hbm, layout),
+        (coupling_hbm, coupling),
+        (matching_hbm, matching),
+        (weights_hbm, weights),
+        (modes_hbm, modes),
+        (clocking_hbm, clocking),
+    ]
+    in_copies = [
+        pltpu.make_async_copy(src, dst, in_sem.at[i]) for i, (src, dst) in enumerate(pairs)
+    ]
+    for copy in in_copies:
+        copy.start()
     for copy in first_copies:
         copy.start()
 
@@ -87,6 +110,7 @@
         pl.semaphore_signal(barrier, inc=1, device_id=(far, h), device_id_type=MESH)
 
     pad[...] = jnp.zeros_like(pad)
+    in_copies[0].wait()
     for h in range(harms):
         for r in range(rows):
             pad[h * rows + r, 0:own_hc, :] = adj[:, h * rows + r, :]
@@ -119,6 +143,8 @@
 
     a_recv[my_h] = a_send[my_h]
 
+    for copy in in_copies[1:]:
+        copy.wait()
     row_id = lax.broadcasted_iota(jnp.int32, (hc, LANES), 0)
     lane_id = lax.broadcasted_iota(jnp.int32, (hc, LANES), 1)
     mode = jnp.zeros((hc, LANES), jnp.float32)
@@ -146,6 +172,8 @@
                 total = term if total is None else total + term
         return total
 
+    for copy in first_copies:
+        copy.wait()
     for h in range(harms):
         @pl.when(other(h))
         def _():
@@ -154,10 +182,9 @@
         for h in range(harms):
             full[r, h * own_hc : (h + 1) * own_hc, :] = a_recv[h, r].astype(jnp.float32)[0:own_hc]
 
-    def products(vectors, blocks, copies):
+    def products(vectors, blocks):
         for r in range(rows):
             for k in range(kk):
-                copies[r * kk + k].wait()
                 terms[r * kk + k] = jnp.dot(
                     vectors[r], blocks[r, k], preferred_element_type=jnp.float32
                 )
@@ -217,7 +244,7 @@
     start1, collect1, drain1 = exchange(send1, recv1, s1_sem, r1_sem)
     start2, collect2, drain2 = exchange(send2, recv2, s2_sem, r2_sem)
 
-    products([full[r].astype(jnp.bfloat16) for r in range(rows)], first_j, first_copies)
+    products([full[r].astype(jnp.bfloat16) for r in range(rows)], first_j)
     for d in (-1, 1, 0):
         for h in range(harms):
             for r in range(rows):
@@ -250,26 +277,33 @@
                 preferred_element_type=jnp.float32,
             )
         )
+    for copy in second_copies:
+        copy.wait()
+    for r in range(rows):
+        tail = plain[r][:, LANES:].astype(jnp.bfloat16)
+        for k in range(kk):
+            terms[r * kk + k] = jnp.dot(
+                tail, second_j[r, k, LANES:, :], preferred_element_type=jnp.float32
+            )
     for h in range(harms):
         m_copy(h, h).wait_recv()
-    coupled = []
     for r in range(rows):
         mortar = jnp.zeros((hc, LANES), jnp.float32)
         for h in range(harms):
             for q in range(rows):
                 place = h * rows + q
-                weight = jnp.where(matching[base + r, 0] == place, weights[base + r, 0], 0.0)
-                weight = weight + jnp.where(matching[base + r, 1] == place, weights[base + r, 1], 0.0)
+                weight = jnp.where(matching[0, base + r] == place, weights[0, base + r], 0.0)
+                weight = weight + jnp.where(matching[1, base + r] == place, weights[1, base + r], 0.0)
                 mortar = mortar + weight * m_recv[h, q]
         swap[r, 0:half, :] = mortar[half:]
         swap[r, half:, :] = mortar[0:half]
         rotated = cosines[r] * mortar + sines[r] * swap[r]
-        head = plain[r][:, 0:LANES] + rotated
-        coupled.append(
-            jnp.concatenate([head, plain[r][:, LANES:]], axis=1).astype(jnp.bfloat16)
-        )
-
-    products(coupled, second_j, second_copies)
+        head = (plain[r][:, 0:LANES] + rotated).astype(jnp.bfloat16)
+        for k in range(kk):
+            terms[r * kk + k] += jnp.dot(
+                head, second_j[r, k, 0:LANES, :], preferred_element_type=jnp.float32
+            )
+
     for d in (-1, 1, 0):
         for s in range(group):
             value = fold((d + 1) * group + s)
@@ -309,16 +343,22 @@
     hc = coupling.shape[0]
     padded = -(-own_hc // 16) * 16
     vmem = pl.BlockSpec(memory_space=pltpu.VMEM)
-    smem = pl.BlockSpec(memory_space=pltpu.SMEM)
     hbm = pl.BlockSpec(memory_space=pl.ANY)
     f32, bf16 = jnp.float32, jnp.bfloat16
     dma = pltpu.SemaphoreType.DMA
     second = pl.pallas_call(
         functools.partial(kernel, tiles, harms),
         out_shape=jax.ShapeDtypeStruct((group * own_hc, width), f32),
-        in_specs=[vmem, smem, vmem, smem, smem, smem, smem, hbm, hbm],
+        in_specs=[hbm] * 9,
         out_specs=vmem,
         scratch_shapes=[
+            pltpu.VMEM(adjoint.shape, f32),
+            pltpu.SMEM(block_column_layout.shape, jnp.int32),
+            pltpu.VMEM(coupling.shape, f32),
+            pltpu.SMEM(matching.shape[::-1], jnp.int32),
+            pltpu.SMEM(intersection.shape[::-1], f32),
+            pltpu.SMEM(modes.shape, jnp.int32),
+            pltpu.SMEM(clocking.shape, f32),
             pltpu.VMEM(first_jacobian_blocks.shape, bf16),
             pltpu.VMEM(first_jacobian_blocks.shape, bf16),
             pltpu.VMEM((group, padded, width), f32),
@@ -333,6 +373,7 @@
             pltpu.VMEM((rows, hc, LANES), f32),
             pltpu.VMEM((3 * harms, group * own_hc, width), f32),
             pltpu.VMEM((3 * harms, group * own_hc, width), f32),
+            dma((7,)),
             dma((rows * kk,)),
             dma((rows * kk,)),
             dma((harms,)),
@@ -345,14 +386,14 @@
             dma((3 * harms,)),
         ],
         compiler_params=pltpu.CompilerParams(
-            collective_id=0, has_side_effects=True, vmem_limit_bytes=40 * 1024 * 1024
+            collective_id=0, has_side_effects=True, vmem_limit_bytes=VMEM_BYTES
         ),
     )(
         adjoint,
         block_column_layout,
         coupling,
-        matching,
-        intersection,
+        matching.T,
+        intersection.T,
         modes,
         clocking,
         first_jacobian_blocks,

time: 39.6 us -> 27.3 us (0.69)
  local copies, waits for them, and re-layouts: 8.87 us -> 1.56 us
  Pallas kernels: 30.3 us -> 25.5 us
    unnamed x18 -> x2, local copies, waits for them, and re-layouts: 8.2 us -> 0.01 us
    pallas_call x1, Pallas kernels: 30.3 us -> 25.5 us  [local(): pl.pallas_call(functools.partial(kernel, tiles, harms), out_shape=jax.Sha...]
    reshape x1, local copies, waits for them, and re-layouts: 0.01 us -> 0.89 us  [local(): second.reshape(group, own_hc, width)]
where the time goes in v2:
time: 27.3 us; the launch traced here: 27.1 us
  Pallas kernels  25.5 us (93%)
  local copies, waits for them, and re-layouts  1.56 us (6%)
    pallas_call x1, Pallas kernels, local(): pl.pallas_call(functools.partial(kernel, tiles, harms), out_shape=jax.Sha...  25.5 us
    reshape x1, local copies, waits for them, and re-layouts, local(): second.reshape(group, own_hc, width)  0.89 us
    sub x1, local copies, waits for them, and re-layouts, local(): objective_grad - jnp.transpose(second.reshape(group, own_hc, width), (1,...  0.66 us

profile of v2, /device:TPU:0, one launch (start us, length us, event | category | flops | bytes accessed | tf_op | source)
XLA Modules:
  0.0 27.1 jit_solution(5294630930681963818)
XLA Ops:
  0.0 0.0 copy-start
  0.0 25.5 %shard_map.100 = f32[48,320]{1,0:T(8,128)} custom-call(f32[12,4,320]{2,1,0:T(4,128)} %adj_hbm.1, s32[4,4]{1,0:T(4,128)} %layout_hbm.1, f32[24,24]{1,0:T(8,128)} %coupling_hbm.1, s32[2,4]{1,0:T(2,128)} %bitcast.4, f32[2,4]{1,0:T(2,128)} %bitcast.5, s32[12]{0:T(128)} %modes_hbm.1, f32[4]{0:T(128)} %clocking_hbm.1, bf16[2,4,320,320]{3,2,1,0:T(8,128)(2,1)} %first_hbm.1, ...), custom_call_target="tpu_custom_call" | custom-call | tf_op jit(solution)/shard_map/pallas_call | solution.py:349
  25.5 0.9 %reshape.3 = f32[4,12,320]{2,1,0:T(8,128)S(1)} reshape(f32[48,320]{1,0:T(8,128)} %shard_map.100) | data formatting | bytes 122880 | tf_op jit(solution)/shard_map/reshape | solution.py:402
  26.4 0.0 copy-done
  26.4 0.7 %copy.13 = f32[12,4,320]{2,1,0:T(4,128)} copy(f32[12,4,320]{2,0,1:T(8,128)S(1)} %bitcast_subtract_fusion) | data formatting | bytes 122880 | tf_op jit(solution)/shard_map/sub | solution.py:402
  (1 shorter events, 0.0 us)
Async XLA Ops:
  0.0 26.4 %copy-start = (f32[12,4,320]{2,1,0:T(4,128)S(1)}, f32[12,4,320]{2,1,0:T(4,128)}, u32[]{:S(2)}) copy-start(f32[12,4,320]{2,1,0:T(4,128)} %param.11) | copy-start | bytes 184324

commit v3 on v2

--- a/solution.py
+++ b/solution.py
@@ -25,6 +25,7 @@
     weights_hbm,
     modes_hbm,
     clocking_hbm,
+    grad_hbm,
     first_hbm,
     second_hbm,
     out,
@@ -35,6 +36,7 @@
     weights,
     modes,
     clocking,
+    grad,
     first_j,
     second_j,
     pad,
@@ -47,6 +49,7 @@
     m_send,
     m_recv,
     swap,
+    stage,
     send2,
     recv2,
     in_sem,
@@ -71,6 +74,18 @@
     far = lax.rem(my_t + tiles // 2, tiles)
     near = [lax.rem(my_t + tiles - 1, tiles), my_t, lax.rem(my_t + 1, tiles)]
 
+    barrier = pltpu.get_barrier_semaphore()
+    for d in (-1, 0, 1):
+        for h in range(harms):
+            if d == 0:
+                @pl.when(h != my_h)
+                def _():
+                    pl.semaphore_signal(barrier, inc=1, device_id=(my_t, h), device_id_type=MESH)
+            else:
+                pl.semaphore_signal(barrier, inc=1, device_id=(near[d + 1], h), device_id_type=MESH)
+    for h in range(harms):
+        pl.semaphore_signal(barrier, inc=1, device_id=(far, h), device_id_type=MESH)
+
     def block_copies(hbm, vmem, sem):
         return [
             pltpu.make_async_copy(hbm.at[r, k], vmem.at[r, k], sem.at[r * kk + k])
@@ -88,6 +103,7 @@
         (weights_hbm, weights),
         (modes_hbm, modes),
         (clocking_hbm, clocking),
+        (grad_hbm, grad),
     ]
     in_copies = [
         pltpu.make_async_copy(src, dst, in_sem.at[i]) for i, (src, dst) in enumerate(pairs)
@@ -96,18 +112,6 @@
         copy.start()
     for copy in first_copies:
         copy.start()
-
-    barrier = pltpu.get_barrier_semaphore()
-    for d in (-1, 0, 1):
-        for h in range(harms):
-            if d == 0:
-                @pl.when(h != my_h)
-                def _():
-                    pl.semaphore_signal(barrier, inc=1, device_id=(my_t, h), device_id_type=MESH)
-            else:
-                pl.semaphore_signal(barrier, inc=1, device_id=(near[d + 1], h), device_id_type=MESH)
-    for h in range(harms):
-        pl.semaphore_signal(barrier, inc=1, device_id=(far, h), device_id_type=MESH)
 
     pad[...] = jnp.zeros_like(pad)
     in_copies[0].wait()
@@ -226,17 +230,17 @@
                     else:
                         copy(d, h, (d + 1) * harms + h).wait_send()
 
-        def collect():
-            total = send[harms + my_h]
+        def collect(total):
             for d in (-1, 1, 0):
                 for h in range(harms):
                     finish(d, h)
                 if d == 0:
                     for j in range(1, harms):
-                        total = total + recv[harms + lax.rem(my_h + j, harms)]
+                        slot = harms + lax.rem(my_h + j, harms)
+                        total = total + recv[slot].astype(jnp.float32)
                 else:
                     for h in range(harms):
-                        total = total + recv[(d + 1) * harms + h]
+                        total = total + recv[(d + 1) * harms + h].astype(jnp.float32)
             return total
 
         return start, collect, drain
@@ -250,9 +254,15 @@
             for r in range(rows):
                 send1[(d + 1) * harms + h, r] = fold((d + 1) * group + h * rows + r)
             start1(d, h)
-    first = collect1()
-
-    m_send[...] = first[:, :, 0:LANES]
+    first = collect1(send1[harms + my_h])
+
+    gap = LANES // rows
+    assert gap >= STRIP
+    packed = first[0][:, 0:LANES]
+    for r in range(1, rows):
+        moved = pltpu.roll(first[r][:, 0:LANES], r * gap, 1)
+        packed = jnp.where(lane_id >= r * gap, moved, packed)
+    m_send[...] = packed
 
     def m_copy(to, slot):
         return pltpu.make_async_remote_copy(
@@ -289,12 +299,14 @@
         m_copy(h, h).wait_recv()
     for r in range(rows):
         mortar = jnp.zeros((hc, LANES), jnp.float32)
-        for h in range(harms):
-            for q in range(rows):
+        for q in range(rows):
+            part = jnp.zeros((hc, LANES), jnp.float32)
+            for h in range(harms):
                 place = h * rows + q
                 weight = jnp.where(matching[0, base + r] == place, weights[0, base + r], 0.0)
                 weight = weight + jnp.where(matching[1, base + r] == place, weights[1, base + r], 0.0)
-                mortar = mortar + weight * m_recv[h, q]
+                part = part + weight * m_recv[h]
+            mortar = mortar + (part if q == 0 else pltpu.roll(part, LANES - q * gap, 1))
         swap[r, 0:half, :] = mortar[half:]
         swap[r, half:, :] = mortar[0:half]
         rotated = cosines[r] * mortar + sines[r] * swap[r]
@@ -308,12 +320,15 @@
         for s in range(group):
             value = fold((d + 1) * group + s)
             for h in range(harms):
-                send2[(d + 1) * harms + h, s * own_hc : (s + 1) * own_hc, :] = value[
+                stage[h, s * own_hc : (s + 1) * own_hc, :] = value[
                     h * own_hc : (h + 1) * own_hc
                 ]
         for h in range(harms):
+            send2[(d + 1) * harms + h] = stage[h].astype(jnp.bfloat16)
             start2(d, h)
-    out[...] = collect2()
+    second = collect2(stage[my_h])
+    for s in range(group):
+        out[:, s, :] = grad[:, s, :] - second[s * own_hc : (s + 1) * own_hc]
 
     for h in range(harms):
         @pl.when(other(h))
@@ -346,10 +361,10 @@
     hbm = pl.BlockSpec(memory_space=pl.ANY)
     f32, bf16 = jnp.float32, jnp.bfloat16
     dma = pltpu.SemaphoreType.DMA
-    second = pl.pallas_call(
+    return pl.pallas_call(
         functools.partial(kernel, tiles, harms),
-        out_shape=jax.ShapeDtypeStruct((group * own_hc, width), f32),
-        in_specs=[hbm] * 9,
+        out_shape=jax.ShapeDtypeStruct(objective_grad.shape, f32),
+        in_specs=[hbm] * 10,
         out_specs=vmem,
         scratch_shapes=[
             pltpu.VMEM(adjoint.shape, f32),
@@ -359,6 +374,7 @@
             pltpu.SMEM(intersection.shape[::-1], f32),
             pltpu.SMEM(modes.shape, jnp.int32),
             pltpu.SMEM(clocking.shape, f32),
+            pltpu.VMEM(objective_grad.shape, f32),
             pltpu.VMEM(first_jacobian_blocks.shape, bf16),
             pltpu.VMEM(first_jacobian_blocks.shape, bf16),
             pltpu.VMEM((group, padded, width), f32),
@@ -368,12 +384,13 @@
             pltpu.VMEM((rows * kk, hc, width), f32),
             pltpu.VMEM((3 * harms, rows, hc, width), f32),
             pltpu.VMEM((3 * harms, rows, hc, width), f32),
+            pltpu.VMEM((hc, LANES), f32),
+            pltpu.VMEM((harms, hc, LANES), f32),
             pltpu.VMEM((rows, hc, LANES), f32),
-            pltpu.VMEM((harms, rows, hc, LANES), f32),
-            pltpu.VMEM((rows, hc, LANES), f32),
-            pltpu.VMEM((3 * harms, group * own_hc, width), f32),
-            pltpu.VMEM((3 * harms, group * own_hc, width), f32),
-            dma((7,)),
+            pltpu.VMEM((harms, group * own_hc, width), f32),
+            pltpu.VMEM((3 * harms, group * own_hc, width), bf16),
+            pltpu.VMEM((3 * harms, group * own_hc, width), bf16),
+            dma((8,)),
             dma((rows * kk,)),
             dma((rows * kk,)),
             dma((harms,)),
@@ -396,10 +413,10 @@
         intersection.T,
         modes,
         clocking,
+        objective_grad,
         first_jacobian_blocks,
         second_jacobian_blocks,
     )
-    return objective_grad - jnp.transpose(second.reshape(group, own_hc, width), (1, 0, 2))
 
 
 def solution(mesh):

time: 27.3 us -> 25.4 us (0.930)
  Pallas kernels: 25.5 us -> 23.7 us
    pallas_call x1, Pallas kernels: 25.5 us -> 23.7 us  [local(): pl.pallas_call(functools.partial(kernel, tiles, harms), out_shape=jax.Sha...]
    unnamed x2 -> x1, local copies, waits for them, and re-layouts: 0.01 us -> 1.52 us
    reshape x1 -> x0, local copies, waits for them, and re-layouts: 0.89 us -> none  [local(): second.reshape(group, own_hc, width)]
    sub x1 -> x0, local copies, waits for them, and re-layouts: 0.66 us -> none  [local(): objective_grad - jnp.transpose(second.reshape(group, own_hc, width), (1,...]
where the time goes in v3:
time: 25.4 us; the launch traced here: 25.3 us
  Pallas kernels  23.7 us (93%)
  local copies, waits for them, and re-layouts  1.52 us (6%)
    pallas_call x1, Pallas kernels, local(): pl.pallas_call(functools.partial(kernel, tiles, harms), out_shape=jax.Sha...  23.7 us
    unnamed x1, local copies, waits for them, and re-layouts  1.52 us

profile of v3, /device:TPU:0, one launch (start us, length us, event | category | flops | bytes accessed | tf_op | source)
XLA Modules:
  0.0 25.3 jit_solution(14989511528464651221)
XLA Ops:
  0.0 23.7 %shard_map.100 = f32[12,4,320]{2,1,0:T(4,128)} custom-call(f32[12,4,320]{2,1,0:T(4,128)} %adj_hbm.1, s32[4,4]{1,0:T(4,128)} %layout_hbm.1, f32[24,24]{1,0:T(8,128)} %coupling_hbm.1, s32[2,4]{1,0:T(2,128)} %bitcast.2, f32[2,4]{1,0:T(2,128)} %bitcast.3, s32[12]{0:T(128)} %modes_hbm.1, f32[4]{0:T(128)} %clocking_hbm.1, f32[12,4,320]{2,1,0:T(4,128)} %grad_hbm.1, ...), custom_call_target="tpu_custom_call" | custom-call | tf_op jit(solution)/shard_map/pallas_call | solution.py:364
  23.7 1.5 %copy.12 = f32[12,4,320]{2,1,0:T(4,128)} copy(f32[12,4,320]{2,1,0:T(4,128)} %shard_map.100) | data formatting | bytes 122880

commit v4 on v3

--- a/solution.py
+++ b/solution.py
@@ -25,7 +25,6 @@
     weights_hbm,
     modes_hbm,
     clocking_hbm,
-    grad_hbm,
     first_hbm,
     second_hbm,
     out,
@@ -36,7 +35,6 @@
     weights,
     modes,
     clocking,
-    grad,
     first_j,
     second_j,
     pad,
@@ -44,8 +42,10 @@
     a_recv,
     full,
     terms,
-    send1,
-    recv1,
+    send1a,
+    recv1a,
+    send1b,
+    recv1b,
     m_send,
     m_recv,
     swap,
@@ -57,8 +57,10 @@
     j2_sem,
     a_ssem,
     a_rsem,
-    s1_sem,
-    r1_sem,
+    s1a_sem,
+    r1a_sem,
+    s1b_sem,
+    r1b_sem,
     m_ssem,
     m_rsem,
     s2_sem,
@@ -103,7 +105,6 @@
         (weights_hbm, weights),
         (modes_hbm, modes),
         (clocking_hbm, clocking),
-        (grad_hbm, grad),
     ]
     in_copies = [
         pltpu.make_async_copy(src, dst, in_sem.at[i]) for i, (src, dst) in enumerate(pairs)
@@ -168,11 +169,11 @@
     def one(r, k, slot):
         return jnp.where(spot[r][k] == slot, 1.0, 0.0).astype(jnp.float32)
 
-    def fold(slot):
+    def fold(slot, low, high):
         total = None
         for r in range(rows):
             for k in range(kk):
-                term = one(r, k, slot) * terms[r * kk + k]
+                term = one(r, k, slot) * terms[r * kk + k, :, low:high]
                 total = term if total is None else total + term
         return total
 
@@ -185,13 +186,6 @@
     for r in range(rows):
         for h in range(harms):
             full[r, h * own_hc : (h + 1) * own_hc, :] = a_recv[h, r].astype(jnp.float32)[0:own_hc]
-
-    def products(vectors, blocks):
-        for r in range(rows):
-            for k in range(kk):
-                terms[r * kk + k] = jnp.dot(
-                    vectors[r], blocks[r, k], preferred_element_type=jnp.float32
-                )
 
     def exchange(send, recv, ssem, rsem):
         def copy(d, to, slot):
@@ -245,22 +239,32 @@
 
         return start, collect, drain
 
-    start1, collect1, drain1 = exchange(send1, recv1, s1_sem, r1_sem)
+    start1a, collect1a, drain1a = exchange(send1a, recv1a, s1a_sem, r1a_sem)
+    start1b, collect1b, drain1b = exchange(send1b, recv1b, s1b_sem, r1b_sem)
     start2, collect2, drain2 = exchange(send2, recv2, s2_sem, r2_sem)
 
-    products([full[r].astype(jnp.bfloat16) for r in range(rows)], first_j)
-    for d in (-1, 1, 0):
-        for h in range(harms):
-            for r in range(rows):
-                send1[(d + 1) * harms + h, r] = fold((d + 1) * group + h * rows + r)
-            start1(d, h)
-    first = collect1(send1[harms + my_h])
+    vectors = [full[r].astype(jnp.bfloat16) for r in range(rows)]
+    for low, high, send, start in ((0, LANES, send1a, start1a), (LANES, width, send1b, start1b)):
+        for r in range(rows):
+            for k in range(kk):
+                terms[r * kk + k, :, low:high] = jnp.dot(
+                    vectors[r],
+                    first_j[r, k, :, low:high],
+                    preferred_element_type=jnp.float32,
+                )
+        for d in (-1, 1, 0):
+            for h in range(harms):
+                for r in range(rows):
+                    slot = (d + 1) * group + h * rows + r
+                    send[(d + 1) * harms + h, r] = fold(slot, low, high)
+                start(d, h)
+    first_head = collect1a(send1a[harms + my_h])
 
     gap = LANES // rows
     assert gap >= STRIP
-    packed = first[0][:, 0:LANES]
+    packed = first_head[0]
     for r in range(1, rows):
-        moved = pltpu.roll(first[r][:, 0:LANES], r * gap, 1)
+        moved = pltpu.roll(first_head[r], r * gap, 1)
         packed = jnp.where(lane_id >= r * gap, moved, packed)
     m_send[...] = packed
 
@@ -276,21 +280,22 @@
 
     for h in range(harms):
         m_copy(h, my_h).start()
-    plain = []
-    for r in range(rows):
-        plain.append(
-            first[r]
-            + jnp.dot(
-                coupling[...],
-                first[r],
-                precision=lax.Precision.HIGHEST,
-                preferred_element_type=jnp.float32,
-            )
+
+    def mix(part):
+        mixed = jnp.dot(
+            coupling[...],
+            part,
+            precision=lax.Precision.HIGHEST,
+            preferred_element_type=jnp.float32,
         )
+        return part + mixed
+
+    plain_head = [mix(first_head[r]) for r in range(rows)]
+    first_tail = collect1b(send1b[harms + my_h])
     for copy in second_copies:
         copy.wait()
     for r in range(rows):
-        tail = plain[r][:, LANES:].astype(jnp.bfloat16)
+        tail = mix(first_tail[r]).astype(jnp.bfloat16)
         for k in range(kk):
             terms[r * kk + k] = jnp.dot(
                 tail, second_j[r, k, LANES:, :], preferred_element_type=jnp.float32
@@ -310,7 +315,7 @@
         swap[r, 0:half, :] = mortar[half:]
         swap[r, half:, :] = mortar[0:half]
         rotated = cosines[r] * mortar + sines[r] * swap[r]
-        head = (plain[r][:, 0:LANES] + rotated).astype(jnp.bfloat16)
+        head = (plain_head[r] + rotated).astype(jnp.bfloat16)
         for k in range(kk):
             terms[r * kk + k] += jnp.dot(
                 head, second_j[r, k, 0:LANES, :], preferred_element_type=jnp.float32
@@ -318,7 +323,7 @@
 
     for d in (-1, 1, 0):
         for s in range(group):
-            value = fold((d + 1) * group + s)
+            value = fold((d + 1) * group + s, 0, width)
             for h in range(harms):
                 stage[h, s * own_hc : (s + 1) * own_hc, :] = value[
                     h * own_hc : (h + 1) * own_hc
@@ -328,14 +333,15 @@
             start2(d, h)
     second = collect2(stage[my_h])
     for s in range(group):
-        out[:, s, :] = grad[:, s, :] - second[s * own_hc : (s + 1) * own_hc]
+        out[:, s, :] = second[s * own_hc : (s + 1) * own_hc]
 
     for h in range(harms):
         @pl.when(other(h))
         def _():
             a_copy(h, h, h).wait_send()
         m_copy(h, h).wait_send()
-    drain1()
+    drain1a()
+    drain1b()
     drain2()
 
 
@@ -361,10 +367,10 @@
     hbm = pl.BlockSpec(memory_space=pl.ANY)
     f32, bf16 = jnp.float32, jnp.bfloat16
     dma = pltpu.SemaphoreType.DMA
-    return pl.pallas_call(
+    second = pl.pallas_call(
         functools.partial(kernel, tiles, harms),
         out_shape=jax.ShapeDtypeStruct(objective_grad.shape, f32),
-        in_specs=[hbm] * 10,
+        in_specs=[hbm] * 9,
         out_specs=vmem,
         scratch_shapes=[
             pltpu.VMEM(adjoint.shape, f32),
@@ -374,7 +380,6 @@
             pltpu.SMEM(intersection.shape[::-1], f32),
             pltpu.SMEM(modes.shape, jnp.int32),
             pltpu.SMEM(clocking.shape, f32),
-            pltpu.VMEM(objective_grad.shape, f32),
             pltpu.VMEM(first_jacobian_blocks.shape, bf16),
             pltpu.VMEM(first_jacobian_blocks.shape, bf16),
             pltpu.VMEM((group, padded, width), f32),
@@ -382,19 +387,23 @@
             pltpu.VMEM((harms, rows, padded, width), bf16),
             pltpu.VMEM((rows, hc, width), f32),
             pltpu.VMEM((rows * kk, hc, width), f32),
-            pltpu.VMEM((3 * harms, rows, hc, width), f32),
-            pltpu.VMEM((3 * harms, rows, hc, width), f32),
+            pltpu.VMEM((3 * harms, rows, hc, LANES), f32),
+            pltpu.VMEM((3 * harms, rows, hc, LANES), f32),
+            pltpu.VMEM((3 * harms, rows, hc, width - LANES), f32),
+            pltpu.VMEM((3 * harms, rows, hc, width - LANES), f32),
             pltpu.VMEM((hc, LANES), f32),
             pltpu.VMEM((harms, hc, LANES), f32),
             pltpu.VMEM((rows, hc, LANES), f32),
             pltpu.VMEM((harms, group * own_hc, width), f32),
             pltpu.VMEM((3 * harms, group * own_hc, width), bf16),
             pltpu.VMEM((3 * harms, group * own_hc, width), bf16),
-            dma((8,)),
+            dma((7,)),
             dma((rows * kk,)),
             dma((rows * kk,)),
             dma((harms,)),
             dma((harms,)),
+            dma((3 * harms,)),
+            dma((3 * harms,)),
             dma((3 * harms,)),
             dma((3 * harms,)),
             dma((harms,)),
@@ -413,10 +422,10 @@
         intersection.T,
         modes,
         clocking,
-        objective_grad,
         first_jacobian_blocks,
         second_jacobian_blocks,
     )
+    return objective_grad - second
 
 
 def solution(mesh):

time: 25.4 us -> 23.7 us (0.933)
  Pallas kernels: 23.7 us -> 21.9 us
  other arithmetic: 0 us -> 1.54 us
  local copies, waits for them, and re-layouts: 1.52 us -> 0.01 us
    pallas_call x1, Pallas kernels: 23.7 us -> 21.9 us  [local(): pl.pallas_call(functools.partial(kernel, tiles, harms), out_shape=jax.Sha...]
    sub x0 -> x1, other arithmetic: none -> 1.54 us  [local(): return objective_grad - second]
    unnamed x1 -> x2, local copies, waits for them, and re-layouts: 1.52 us -> 0.01 us
where the time goes in v4:
time: 23.7 us; the launch traced here: 23.5 us
  Pallas kernels  21.9 us (92%)
  other arithmetic  1.54 us (6%)
    pallas_call x1, Pallas kernels, local(): pl.pallas_call(functools.partial(kernel, tiles, harms), out_shape=jax.Sha...  21.9 us
    sub x1, other arithmetic, local(): return objective_grad - second  1.54 us

profile of v4, /device:TPU:0, one launch (start us, length us, event | category | flops | bytes accessed | tf_op | source)
XLA Modules:
  0.0 23.5 jit_solution(4669081778318998136)
XLA Ops:
  0.0 0.0 copy-start
  0.0 21.9 %shard_map.100 = f32[12,4,320]{2,1,0:T(4,128)} custom-call(f32[12,4,320]{2,1,0:T(4,128)} %adj_hbm.1, s32[4,4]{1,0:T(4,128)} %layout_hbm.1, f32[24,24]{1,0:T(8,128)} %coupling_hbm.1, s32[2,4]{1,0:T(2,128)} %bitcast.2, f32[2,4]{1,0:T(2,128)} %bitcast.3, s32[12]{0:T(128)} %modes_hbm.1, f32[4]{0:T(128)} %clocking_hbm.1, bf16[2,4,320,320]{3,2,1,0:T(8,128)(2,1)} %first_hbm.1, ...), custom_call_target="tpu_custom_call" | custom-call | tf_op jit(solution)/shard_map/pallas_call | solution.py:370
  22.0 0.0 copy-done
  22.0 1.5 %sub.3 = f32[12,4,320]{2,1,0:T(4,128)} subtract(f32[12,4,320]{2,1,0:T(4,128)S(1)} %copy-done, f32[12,4,320]{2,1,0:T(4,128)} %shard_map.100) | non-fusion elementwise | flops 15360 | bytes 184320 | tf_op jit(solution)/shard_map/sub | solution.py:428
Async XLA Ops:
  0.0 22.0 %copy-start = (f32[12,4,320]{2,1,0:T(4,128)S(1)}, f32[12,4,320]{2,1,0:T(4,128)}, u32[]{:S(2)}) copy-start(f32[12,4,320]{2,1,0:T(4,128)} %param.11) | copy-start | bytes 184324

commit v5 on v4

--- a/solution.py
+++ b/solution.py
@@ -44,6 +44,7 @@
     terms,
     send1a,
     recv1a,
+    stage1,
     send1b,
     recv1b,
     m_send,
@@ -256,8 +257,15 @@
             for h in range(harms):
                 for r in range(rows):
                     slot = (d + 1) * group + h * rows + r
-                    send[(d + 1) * harms + h, r] = fold(slot, low, high)
+                    if low == 0:
+                        send[(d + 1) * harms + h, r] = fold(slot, low, high)
+                    else:
+                        stage1[r * hc : (r + 1) * hc, :] = fold(slot, low, high)
+                if low > 0:
+                    send[(d + 1) * harms + h] = stage1[...].astype(jnp.bfloat16)
                 start(d, h)
+    for r in range(rows):
+        stage1[r * hc : (r + 1) * hc, :] = fold(group + my_h * rows + r, LANES, width)
     first_head = collect1a(send1a[harms + my_h])
 
     gap = LANES // rows
@@ -291,11 +299,11 @@
         return part + mixed
 
     plain_head = [mix(first_head[r]) for r in range(rows)]
-    first_tail = collect1b(send1b[harms + my_h])
+    first_tail = collect1b(stage1[...])
     for copy in second_copies:
         copy.wait()
     for r in range(rows):
-        tail = mix(first_tail[r]).astype(jnp.bfloat16)
+        tail = mix(first_tail[r * hc : (r + 1) * hc]).astype(jnp.bfloat16)
         for k in range(kk):
             terms[r * kk + k] = jnp.dot(
                 tail, second_j[r, k, LANES:, :], preferred_element_type=jnp.float32
@@ -389,8 +397,9 @@
             pltpu.VMEM((rows * kk, hc, width), f32),
             pltpu.VMEM((3 * harms, rows, hc, LANES), f32),
             pltpu.VMEM((3 * harms, rows, hc, LANES), f32),
-            pltpu.VMEM((3 * harms, rows, hc, width - LANES), f32),
-            pltpu.VMEM((3 * harms, rows, hc, width - LANES), f32),
+            pltpu.VMEM((rows * hc, width - LANES), f32),
+            pltpu.VMEM((3 * harms, rows * hc, width - LANES), bf16),
+            pltpu.VMEM((3 * harms, rows * hc, width - LANES), bf16),
             pltpu.VMEM((hc, LANES), f32),
             pltpu.VMEM((harms, hc, LANES), f32),
             pltpu.VMEM((rows, hc, LANES), f32),

time: 23.7 us -> 23.3 us (0.983)
  Pallas kernels: 21.9 us -> 21.6 us
    pallas_call x1, Pallas kernels: 21.9 us -> 21.6 us  [local(): pl.pallas_call(functools.partial(kernel, tiles, harms), out_shape=jax.Sha...]
where the time goes in v5:
time: 23.3 us; the launch traced here: 23.1 us
  Pallas kernels  21.6 us (93%)
  other arithmetic  1.54 us (7%)
    pallas_call x1, Pallas kernels, local(): pl.pallas_call(functools.partial(kernel, tiles, harms), out_shape=jax.Sha...  21.6 us
    sub x1, other arithmetic, local(): return objective_grad - second  1.54 us

profile of v5, /device:TPU:0, one launch (start us, length us, event | category | flops | bytes accessed | tf_op | source)
XLA Modules:
  0.0 23.1 jit_solution(6004135141524759450)
XLA Ops:
  0.0 0.0 copy-start
  0.0 21.6 %shard_map.100 = f32[12,4,320]{2,1,0:T(4,128)} custom-call(f32[12,4,320]{2,1,0:T(4,128)} %adj_hbm.1, s32[4,4]{1,0:T(4,128)} %layout_hbm.1, f32[24,24]{1,0:T(8,128)} %coupling_hbm.1, s32[2,4]{1,0:T(2,128)} %bitcast.2, f32[2,4]{1,0:T(2,128)} %bitcast.3, s32[12]{0:T(128)} %modes_hbm.1, f32[4]{0:T(128)} %clocking_hbm.1, bf16[2,4,320,320]{3,2,1,0:T(8,128)(2,1)} %first_hbm.1, ...), custom_call_target="tpu_custom_call" | custom-call | tf_op jit(solution)/shard_map/pallas_call | solution.py:378
  21.6 0.0 copy-done
  21.6 1.5 %sub.3 = f32[12,4,320]{2,1,0:T(4,128)} subtract(f32[12,4,320]{2,1,0:T(4,128)S(1)} %copy-done, f32[12,4,320]{2,1,0:T(4,128)} %shard_map.100) | non-fusion elementwise | flops 15360 | bytes 184320 | tf_op jit(solution)/shard_map/sub | solution.py:437
Async XLA Ops:
  0.0 21.6 %copy-start = (f32[12,4,320]{2,1,0:T(4,128)S(1)}, f32[12,4,320]{2,1,0:T(4,128)}, u32[]{:S(2)}) copy-start(f32[12,4,320]{2,1,0:T(4,128)} %param.11) | copy-start | bytes 184324
